TPU v7x, 128 devices: a whole 4x4x4 slice. The times are simulated.
128 devices in a mesh: patch: 32 (over x, y, core), tensor: 2 (over z_lo), guide: 2 (over z_hi).
Axes of the slice: x: 4, y: 4, z: 4 (z_hi: 2, z_lo: 2; z = z_hi * 2 + z_lo), core: 2. Of those that a mesh axis runs over, the one named last changes fastest.
Arguments:
- fresh_q: bfloat16 [2, 6144, 2560], P('guide', 'patch', 'tensor'), may hold values from -61 to 61
- fresh_k: bfloat16 [2, 6144, 2560], P('guide', 'patch', 'tensor'), may hold values from -45 to 45
- fresh_v: bfloat16 [2, 6144, 2560], P('guide', 'patch', 'tensor'), may hold values from -6 to 6
- stale_k: bfloat16 [2, 6144, 2560], P('guide', 'patch', 'tensor'), may hold values from -45 to 45
- stale_v: bfloat16 [2, 6144, 2560], P('guide', 'patch', 'tensor'), may hold values from -6 to 6
- positions: int32 [3, 6144], P(None, 'patch'), may hold values from 0 to 31
- residual: bfloat16 [2, 6144, 5120], P('guide', 'patch', 'tensor'), may hold values from -3 to 3
- out_weight: bfloat16 [2560, 5120], P('tensor'), may hold values from -0.125 to 0.125
- gate_table: float32 [50, 5120], replicated, may hold values from 0.3 to 3
- timestep: int32 [1], replicated, may hold values from 0 to 49
Outputs:
- guided: bfloat16 [6144, 5120], P('patch', ('tensor', 'guide'))
All inputs are finite; a program needn't handle non-finite values.
Results may differ from a plain program's by a relative error of at most 0.011.
Values may be sent and summed in bfloat16 or wider, within the bound.
A program may use at most 128 MiB of HBM per device.

v0:
```python
import math

import jax
import jax.numpy as jnp
from jax import lax
from jax.sharding import PartitionSpec as P

HEAD_DIM = 128


guide_scale = 5.0


def rotate_positions(values, positions):
    rows_count = values.shape[0]
    width = values.shape[1]
    head_count = width // HEAD_DIM
    half_dim = HEAD_DIM // 2
    side_pairs = HEAD_DIM // 6
    frame_pairs = half_dim - 2 * side_pairs
    pair_index = lax.iota(jnp.int32, half_dim)
    section = (pair_index >= frame_pairs).astype(jnp.int32) + (
        pair_index >= frame_pairs + side_pairs
    ).astype(jnp.int32)
    local_index = pair_index - jnp.where(
        section == 0, 0, jnp.where(section == 1, frame_pairs, frame_pairs + side_pairs)
    )
    section_pairs = jnp.where(section == 0, frame_pairs, side_pairs)
    exponent = local_index.astype(jnp.float32) / section_pairs.astype(jnp.float32)
    freqs = jnp.power(jnp.float32(10000.0), -exponent)
    place = positions.astype(jnp.float32)
    chosen = jnp.where(
        section[None, :] == 0,
        place[0][:, None],
        jnp.where(section[None, :] == 1, place[1][:, None], place[2][:, None]),
    )
    angles = chosen * freqs[None, :]
    cosines = jnp.repeat(jnp.cos(angles), 2, axis=1)
    sines = jnp.repeat(jnp.sin(angles), 2, axis=1)
    row_ids = lax.iota(jnp.int32, HEAD_DIM)[:, None]
    col_ids = lax.iota(jnp.int32, HEAD_DIM)[None, :]
    swap_table = jnp.where(
        (row_ids % 2 == 1) & (col_ids == row_ids - 1),
        -1.0,
        jnp.where((row_ids % 2 == 0) & (col_ids == row_ids + 1), 1.0, 0.0),
    ).astype(jnp.float32)
    shaped = values.astype(jnp.float32).reshape(rows_count, head_count, HEAD_DIM)
    turned = jnp.einsum("thd,de->the", shaped, swap_table, precision=lax.Precision.HIGHEST)
    result = shaped * cosines[:, None, :] + turned * sines[:, None, :]
    return result.reshape(rows_count, width)


def update_heads(state_now, queries, keys, values):
    head_count = queries.shape[1] // HEAD_DIM
    score_scale = 1.0 / math.sqrt(HEAD_DIM)

    def one_head(head, state_inner):
        top_all, total_all, summed_all = state_inner
        column = head * HEAD_DIM
        query_head = lax.dynamic_slice_in_dim(queries, column, HEAD_DIM, 1)
        key_head = lax.dynamic_slice_in_dim(keys, column, HEAD_DIM, 1)
        value_head = lax.dynamic_slice_in_dim(values, column, HEAD_DIM, 1)
        scores = (
            lax.dot_general(
                query_head, key_head, (((1,), (1,)), ((), ())), preferred_element_type=jnp.float32
            )
            * score_scale
        )
        top_old = lax.dynamic_index_in_dim(top_all, head, 0, keepdims=False)
        total_old = lax.dynamic_index_in_dim(total_all, head, 0, keepdims=False)
        summed_old = lax.dynamic_index_in_dim(summed_all, head, 0, keepdims=False)
        top_new = jnp.maximum(top_old, jnp.max(scores, axis=1))
        expo = jnp.exp(scores - top_new[:, None])
        fade = jnp.exp(top_old - top_new)
        total_new = total_old * fade + jnp.sum(expo, axis=1)
        summed_new = summed_old * fade[:, None] + jnp.dot(
            expo.astype(jnp.bfloat16), value_head, preferred_element_type=jnp.float32
        )
        return (
            lax.dynamic_update_index_in_dim(top_all, top_new, head, 0),
            lax.dynamic_update_index_in_dim(total_all, total_new, head, 0),
            lax.dynamic_update_index_in_dim(summed_all, summed_new, head, 0),
        )

    return lax.fori_loop(0, head_count, one_head, state_now)


def finish_heads(state_now):
    top_all, total_all, summed_all = state_now
    result = (summed_all / total_all[:, :, None]).astype(jnp.bfloat16)
    head_count = result.shape[0]
    tok_rows = result.shape[1]
    return jnp.transpose(result, (1, 0, 2)).reshape(tok_rows, head_count * HEAD_DIM)


def start_state(head_count, tok_rows):
    return (
        jnp.full((head_count, tok_rows), -jnp.inf, jnp.float32),
        jnp.zeros((head_count, tok_rows), jnp.float32),
        jnp.zeros((head_count, tok_rows, HEAD_DIM), jnp.float32),
    )


def per_device(
    fresh_q,
    fresh_k,
    fresh_v,
    stale_k,
    stale_v,
    positions,
    residual,
    out_weight,
    gate_table,
    timestep,
):
    tok_rows = fresh_q.shape[1]
    width_local = fresh_q.shape[2]
    head_count = width_local // HEAD_DIM
    own_start = lax.axis_index("patch") * tok_rows
    queries = rotate_positions(fresh_q[0], positions).astype(jnp.bfloat16)
    keys_own = rotate_positions(fresh_k[0], positions).astype(jnp.bfloat16)
    values_own = fresh_v[0]
    empty_state = start_state(head_count, tok_rows)
    keys_all, values_all = (
        lax.all_gather(stale_k[0], "patch", axis=0, tiled=True),
        lax.all_gather(stale_v[0], "patch", axis=0, tiled=True),
    )
    keys_all = lax.dynamic_update_slice_in_dim(keys_all, keys_own, own_start, 0)
    values_all = lax.dynamic_update_slice_in_dim(values_all, values_own, own_start, 0)
    attn = finish_heads(update_heads(empty_state, queries, keys_all, values_all))
    partial_value = jnp.dot(attn, out_weight, preferred_element_type=jnp.float32)
    steps_count = gate_table.shape[0]
    one_hot = (lax.iota(jnp.int32, steps_count) == timestep[0]).astype(jnp.float32)[None, :]
    gate_row = jnp.dot(
        one_hot, gate_table, precision=lax.Precision.HIGHEST, preferred_element_type=jnp.float32
    )
    half_cols = residual.shape[2]
    col_start = lax.axis_index("tensor") * half_cols
    summed = lax.psum_scatter(
        partial_value.astype(jnp.bfloat16), "tensor", scatter_dimension=1, tiled=True
    ).astype(jnp.float32)
    gate_half = lax.dynamic_slice_in_dim(gate_row, col_start, half_cols, 1)
    hidden = residual[0].astype(jnp.float32) + gate_half * summed
    both_branches = lax.all_to_all(
        hidden.reshape(tok_rows, 2, half_cols // 2).astype(jnp.bfloat16),
        "guide",
        split_axis=1,
        concat_axis=1,
        tiled=True,
    ).astype(jnp.float32)
    guided = both_branches[:, 1, :] + guide_scale * (
        both_branches[:, 0, :] - both_branches[:, 1, :]
    )
    return guided.astype(jnp.bfloat16)


def solution(mesh):
    in_specs = (
        P("guide", "patch", "tensor"),
        P("guide", "patch", "tensor"),
        P("guide", "patch", "tensor"),
        P("guide", "patch", "tensor"),
        P("guide", "patch", "tensor"),
        P(None, "patch"),
        P("guide", "patch", "tensor"),
        P("tensor", None),
        P(),
        P(),
    )
    out_specs = P("patch", ("tensor", "guide"))
    return jax.shard_map(
        per_device, mesh=mesh, in_specs=in_specs, out_specs=out_specs, check_vma=False
    )
```

profile of v0, /device:TPU:0, one launch (start us, length us, event | category | flops | bytes accessed | tf_op | source)
XLA Modules:
  0.0 282.4 jit_solution(7495926118725498797)
XLA Ops:
  9.6 1.3 copy.18
  11.2 0.9 fusion.33
  12.6 1.3 copy.12
  15.5 66.7 %all-gather.5.cloned.1.call-done = bf16[1,6144,1280]{2,1,0:T(8,128)(2,1)} async-done(((bf16[1,192,1280]{2,1,0:T(8,128)(2,1)}), bf16[1,6144,1280]{2,1,0:T(8,128)(2,1)}) %all-gather.5.cloned.1.call-update) | async-done | bytes 15728656 | tf_op jit(solution)/shard_map/all_gather | solution.py:125
  83.0 71.1 %all-gather.7.cloned.1.call-done = bf16[1,6144,1280]{2,1,0:T(8,128)(2,1)} async-done(((bf16[1,192,1280]{2,1,0:T(8,128)(2,1)}), bf16[1,6144,1280]{2,1,0:T(8,128)(2,1)}) %all-gather.7.cloned.1.call-update) | async-done | bytes 15728656 | tf_op jit(solution)/shard_map/all_gather | solution.py:126
  154.2 1.8 bitcast_dynamic-update-slice_fusion
  156.1 56.7 %while.17 = (s32[]{:T(128)}, f32[10,192]{1,0:T(8,128)S(1)}, f32[10,192]{1,0:T(8,128)S(1)}, f32[10,192,128]{2,1,0:T(8,128)S(1)}, bf16[192,1280]{1,0:T(8,128)(2,1)...) while((s32[]{:T(128)}, f32[10,192]{1,0:T(8,128)S(1)}, ...), condition=%wide.region_3.4_spmd, body=%wide.region_0.3_spmd.sunk | while | flops 611107584 | bytes 17762228 | solution.py:85
  156.1 2.3 fusion.90
  158.5 2.4 fusion.93
  161.8 2.3 fusion.90
  164.1 2.4 fusion.93
  167.5 2.3 fusion.90
  169.8 2.4 fusion.93
  173.1 2.3 fusion.90
  175.5 2.4 fusion.93
  178.8 2.3 fusion.90
  181.1 2.4 fusion.93
  184.5 2.3 fusion.90
  186.8 2.4 fusion.93
  190.1 2.3 fusion.90
  192.5 2.4 fusion.93
  195.8 2.3 fusion.90
  198.2 2.4 fusion.93
  201.5 2.3 fusion.90
  203.8 2.4 fusion.93
  207.1 2.3 fusion.90
  209.5 2.4 fusion.93
  213.4 8.9 %convolution_convert_fusion = bf16[192,5120]{1,0:T(8,128)(2,1)} fusion(bf16[192,1280]{0,1:T(8,128)(2,1)S(1)} %bitcast.100, bf16[1280,5120]{1,0:T(8,128)(2,1)} %param.19), kind=kOutput, calls=%fused_computation.21 | convolution fusion | flops 2517565440 | bytes 15564800 | tf_op jit(solution)/shard_map/dot_general | solution.py:131
  223.5 31.4 %reduce-scatter.2.cloned.1.call-done = bf16[192,2560]{1,0:T(8,128)(2,1)} async-done(((bf16[192,5120]{1,0:T(8,128)(2,1)}), bf16[192,2560]{1,0:T(8,128)(2,1)}) %reduce-scatter.2.cloned.1.call-update) | async-done | bytes 983056 | tf_op jit(solution)/shard_map/reduce_scatter | solution.py:139
  255.0 1.5 fusion.27
  256.5 18.3 %all_to_all.5 = bf16[192,2,1280]{2,0,1:T(8,128)(2,1)S(1)} all-to-all(bf16[192,2,1280]{2,0,1:T(8,128)(2,1)S(1)} %bitcast.97), channel_id=1, replica_groups=mesh['patch'=32,'tensor'=2,'guide'=2] {'guide'}, dimensions={1} | all-to-all | bytes 1966080 | tf_op jit(solution)/shard_map/all_to_all | solution.py:144
  275.0 0.9 fusion.37
  (110 shorter events, 17.0 us)
Async XLA Ops:
  6.5 216.4 %copy-start = (f32[50,5120]{1,0:T(8,128)S(1)}, f32[50,5120]{1,0:T(8,128)}, u32[]{:S(2)}) copy-start(f32[50,5120]{1,0:T(8,128)} %param.20) | copy-start | bytes 3072004
  6.5 75.7 %all-gather.5.cloned.1.call-start = ((), (), s32[]{:S(2)}) async-start(), calls=%async_computation.3 | async-start | bytes 16220160 | tf_op jit(solution)/shard_map/all_gather | solution.py:125
  7.3 146.9 %all-gather.7.cloned.1.call-start = ((), (), s32[]{:S(2)}) async-start(), calls=%async_computation.4 | async-start | bytes 16220160 | tf_op jit(solution)/shard_map/all_gather | solution.py:126
  8.0 246.9 %reduce-scatter.2.cloned.1.call-start = ((), (), s32[]{:S(2)}) async-start(), calls=%async_computation.2 | async-start | bytes 2949120 | tf_op jit(solution)/shard_map/reduce_scatter | solution.py:139
  213.4 41.6 %copy-start.1 = (bf16[1,192,2560]{2,1,0:T(8,128)(2,1)S(1)}, bf16[1,192,2560]{2,1,0:T(8,128)(2,1)}, u32[]{:S(2)}) copy-start(bf16[1,192,2560]{2,1,0:T(8,128)(2,1)} %param.18) | copy-start | bytes 2949124
Sparse Core Ops, SparseCore 0:
  9.6 72.5 all-gather.4
  84.5 69.6 all-gather.6
  222.4 32.5 reduce-scatter.1
where the time goes:
time: 283 us; the launch traced here: 282 us
  waiting for transfers between devices  171 us (60%)
  matrix products  57.7 us (20%)
  blocking collectives  18.3 us (6%)
  between operations  14 us (5%)
  other arithmetic  12.1 us (4%)
  local copies, waits for them, and re-layouts  8.85 us (3%)
    all_gather x1, waiting for transfers between devices, per_device(): lax.all_gather(stale_v[0], 'patch', axis=0, tiled=True)  71.1 us
    all_gather x1, waiting for transfers between devices, per_device(): lax.all_gather(stale_k[0], 'patch', axis=0, tiled=True)  66.7 us
    reduce_scatter x1, waiting for transfers between devices, per_device(): lax.psum_scatter(partial_value.astype(jnp.bfloat16), 'tensor', scatter_di...  31.4 us
    dot_general x10, matrix products, one_head(): jnp.dot(expo.astype(jnp.bfloat16), value_head, preferred_element_type=jnp...  23.8 us
    dot_general x10, matrix products, one_head(): lax.dot_general(query_head, key_head, (((1,), (1,)), ((), ())), preferred...  22.9 us
    all_to_all x1, blocking collectives, per_device(): lax.all_to_all(hidden.reshape(tok_rows, 2, half_cols // 2).astype(jnp.bfl...  18.3 us
    dot_general x1, matrix products, per_device(): jnp.dot(attn, out_weight, preferred_element_type=jnp.float32)  8.88 us
    reduce_sum x10, other arithmetic, one_head(): total_new = total_old * fade + jnp.sum(expo, axis=1)  7.94 us
  transfers between devices with their start and end apart: 3, of which 3 were waited for; matrix products, arithmetic and copies ran while one was open for 3% of the time, Pallas kernels for 0%

commit v1 on v0

v1 whole, which is shorter than its diff:
```python
import functools
import math

import jax
import jax.numpy as jnp
import numpy as np
from jax import lax
from jax.experimental import pallas as pl
from jax.experimental.pallas import tpu as pltpu
from jax.sharding import PartitionSpec as P

MESH = pl.DeviceIdType.MESH
BF = jnp.bfloat16
F32 = jnp.float32
HEAD_DIM = 128
GUIDE_SCALE = 5.0
RING = 4
ROWS = 192
GROUP = 5
HEADS = 10
KEYS = 8 * ROWS
NOTE = 16
HALF = 640
SCORE_SCALE = math.log2(math.e) / math.sqrt(HEAD_DIM)

(K_LEFT, K_RIGHT, V_LEFT, V_RIGHT, K_FAR, V_FAR, Q_LEFT, Q_RIGHT, Q_FAR, SIB_K, SIB_V, SIB_FK, SIB_FV, SIB_Q) = range(14)
KINDS = 14


def frequencies():
    half_dim = HEAD_DIM // 2
    side_pairs = HEAD_DIM // 6
    frame_pairs = half_dim - 2 * side_pairs
    table = np.zeros((8, HEAD_DIM), np.float32)
    for pair in range(half_dim):
        if pair < frame_pairs:
            section, local, size = 0, pair, frame_pairs
        elif pair < frame_pairs + side_pairs:
            section, local, size = 1, pair - frame_pairs, side_pairs
        else:
            section, local, size = 2, pair - frame_pairs - side_pairs, side_pairs
        table[section, 2 * pair : 2 * pair + 2] = 10000.0 ** (-local / size)
    return table


def block_rows(index, count=1):
    return pl.ds(pl.multiple_of(index * ROWS, ROWS), count * ROWS)


def head_columns(head):
    return pl.ds(pl.multiple_of(head * HEAD_DIM, HEAD_DIM), HEAD_DIM)


def same_lane(rows):
    shape = (rows, HEAD_DIM)
    return lax.broadcasted_iota(jnp.int32, shape, 0) == lax.broadcasted_iota(jnp.int32, shape, 1)


def kernel(
    fresh_q, fresh_k, fresh_v, stale_k, stale_v, residual, weight, gate_table, freqs, positions, timestep,
    out,
    kb, vb, qb, q_raw, k_raw, q_rot, k_rot, o_send, o_recv, attn, attn_other, combined, w_tiles, part_send, part_recv,
    part_own, res_own, res_other, gate_rows, cosines, sines,
    recv, o_recv_sem, kv_sem, q_sem, far_sem, sib_sem, local_sem, o_sem, guide_send, guide_recv, part_send_sem,
    part_recv_sem, res_sem, load_sem,
):
    p, t, g = lax.axis_index("patch"), lax.axis_index("tensor"), lax.axis_index("guide")
    x, y, c = p // (2 * RING), (p // 2) % RING, p % 2
    sib = 1 - c

    def at(dx, dy, core):
        return (((x + dx) % RING * RING + (y + dy) % RING) * 2 + core, t, g)

    def send(src, dst, send_sem, recv_sem, device):
        pltpu.make_async_remote_copy(
            src_ref=src, dst_ref=dst, send_sem=send_sem, recv_sem=recv_sem, device_id=device, device_id_type=MESH
        ).start()

    def await_bytes(ref, sem):
        pltpu.make_async_copy(ref, ref, sem).wait()

    def got(kind, i):
        return recv.at[kind * GROUP + i]

    own_slot, fresh_slot = 1 + 7 * c, 9 - 9 * c

    load_q = pltpu.make_async_copy(fresh_q.at[0], q_raw, load_sem.at[0])
    load_k = pltpu.make_async_copy(fresh_k.at[0], k_raw, load_sem.at[1])
    load_q.start()
    load_k.start()

    peers = [at(dx, 0, core) for dx in (1, 3) for core in (0, 1)]
    peers += [at(0, dy, core) for dy in (1, 2, 3) for core in (0, 1)]
    peers += [at(0, 0, sib), (p, 1 - t, g), (p, 1 - t, 1 - g), (p, t, 1 - g)]
    barrier = pltpu.get_barrier_semaphore()
    for peer in peers:
        pl.semaphore_signal(barrier, inc=1, device_id=peer, device_id_type=MESH)

    def local_stale(i, start):
        columns = head_columns(GROUP * c + i)
        copies = (
            pltpu.make_async_copy(stale_k.at[0, :, columns], kb.at[i, block_rows(own_slot), :], local_sem.at[i, 0]),
            pltpu.make_async_copy(stale_v.at[0, :, columns], vb.at[i, block_rows(own_slot), :], local_sem.at[i, 1]),
            pltpu.make_async_copy(fresh_v.at[0, :, columns], vb.at[i, block_rows(fresh_slot), :], local_sem.at[i, 2]),
        )
        for copy in copies:
            copy.start() if start else copy.wait()

    def local_rotated(i, start):
        head = GROUP * c + i
        copies = (
            pltpu.make_async_copy(k_rot.at[head], kb.at[i, block_rows(fresh_slot), :], local_sem.at[i, 3]),
            pltpu.make_async_copy(q_rot.at[head], qb.at[i, block_rows(c), :], local_sem.at[i, 4]),
        )
        for copy in copies:
            copy.start() if start else copy.wait()

    def send_own(i):
        for core in (0, 1):
            columns = head_columns(GROUP * core + i)
            for tensor, (source, buf) in enumerate(((stale_k, kb), (stale_v, vb))):
                for way, (dx, slot, kind) in enumerate(((1, 2, 2 * tensor), (3, 4, 2 * tensor + 1))):
                    send(
                        source.at[0, :, columns],
                        buf.at[i, block_rows(slot + c), :],
                        kv_sem.at[i, core * 4 + tensor * 2 + way],
                        got(kind, i),
                        at(dx, 0, core),
                    )

    def send_sibling_stale(i):
        columns = head_columns(GROUP * sib + i)
        device = at(0, 0, sib)
        send(stale_k.at[0, :, columns], kb.at[i, block_rows(own_slot), :], sib_sem.at[i, 0], got(SIB_K, i), device)
        send(stale_v.at[0, :, columns], vb.at[i, block_rows(own_slot), :], sib_sem.at[i, 1], got(SIB_V, i), device)
        send(fresh_v.at[0, :, columns], vb.at[i, block_rows(fresh_slot), :], sib_sem.at[i, 2], got(SIB_FV, i), device)

    def send_rotated(i):
        head = GROUP * sib + i
        device = at(0, 0, sib)
        send(q_rot.at[head], qb.at[i, block_rows(c), :], sib_sem.at[i, 3], got(SIB_Q, i), device)
        send(k_rot.at[head], kb.at[i, block_rows(fresh_slot), :], sib_sem.at[i, 4], got(SIB_FK, i), device)
        for core in (0, 1):
            for way, (dy, block, kind) in enumerate(((1, 6, Q_LEFT), (3, 2, Q_RIGHT))):
                send(
                    q_rot.at[GROUP * core + i],
                    qb.at[i, block_rows(block + c), :],
                    q_sem.at[i, core * 2 + way],
                    got(kind, i),
                    at(0, dy, core),
                )

    def forward(i):
        await_bytes(kb.at[i, block_rows(2, 2), :], got(K_LEFT, i))
        send(
            kb.at[i, block_rows(2, 2), :], kb.at[i, block_rows(6, 2), :], far_sem.at[i, 0], got(K_FAR, i), at(1, 0, c)
        )
        await_bytes(vb.at[i, block_rows(4, 2), :], got(V_RIGHT, i))
        send(
            vb.at[i, block_rows(4, 2), :], vb.at[i, block_rows(6, 2), :], far_sem.at[i, 1], got(V_FAR, i), at(3, 0, c)
        )
        await_bytes(qb.at[i, block_rows(6, 2), :], got(Q_LEFT, i))
        send(qb.at[i, block_rows(6), :], qb.at[i, block_rows(4), :], far_sem.at[i, 2], got(Q_FAR, i), at(0, 1, c))
        await_bytes(qb.at[i, block_rows(2, 2), :], got(Q_RIGHT, i))
        send(qb.at[i, block_rows(3), :], qb.at[i, block_rows(5), :], far_sem.at[i, 3], got(Q_FAR, i), at(0, 3, c))

    def arrived(i):
        local_stale(i, False)
        local_rotated(i, False)
        other = 8 - 7 * c
        other_fresh = 9 * c
        await_bytes(kb.at[i, block_rows(other), :], got(SIB_K, i))
        await_bytes(vb.at[i, block_rows(other), :], got(SIB_V, i))
        await_bytes(kb.at[i, block_rows(other_fresh), :], got(SIB_FK, i))
        await_bytes(vb.at[i, block_rows(other_fresh), :], got(SIB_FV, i))
        await_bytes(qb.at[i, block_rows(sib), :], got(SIB_Q, i))
        await_bytes(kb.at[i, block_rows(4, 2), :], got(K_RIGHT, i))
        await_bytes(vb.at[i, block_rows(2, 2), :], got(V_LEFT, i))
        await_bytes(kb.at[i, block_rows(6, 2), :], got(K_FAR, i))
        await_bytes(vb.at[i, block_rows(6, 2), :], got(V_FAR, i))
        await_bytes(qb.at[i, block_rows(4, 2), :], got(Q_FAR, i))

    pl.semaphore_wait(barrier, len(peers))
    send_own(0)

    @pl.loop(0, GROUP)
    def _(i):
        local_stale(i, True)
        send_sibling_stale(i)

    res_columns = residual.shape[2] // 2
    mine = pl.ds(pl.multiple_of(g * res_columns, HEAD_DIM), res_columns)
    partner = pl.ds(pl.multiple_of((1 - g) * res_columns, HEAD_DIM), res_columns)

    where_at = positions[...].astype(F32)
    row_of = lax.broadcasted_iota(jnp.int32, (8, ROWS), 0)
    places = jnp.where(
        row_of == 0, where_at[0:1], jnp.where(row_of == 1, where_at[1:2], jnp.where(row_of == 2, where_at[2:3], 0.0))
    )
    angles = lax.dot_general(
        places, freqs[...], (((0,), (0,)), ((), ())), precision=lax.Precision.HIGHEST, preferred_element_type=F32
    )
    cosines[...] = jnp.cos(angles)
    sines[...] = jnp.sin(angles)
    row_ids = lax.broadcasted_iota(jnp.int32, (HEAD_DIM, HEAD_DIM), 0)
    col_ids = lax.broadcasted_iota(jnp.int32, (HEAD_DIM, HEAD_DIM), 1)
    swap = jnp.where(
        (row_ids % 2 == 1) & (col_ids == row_ids - 1),
        -1.0,
        jnp.where((row_ids % 2 == 0) & (col_ids == row_ids + 1), 1.0, 0.0),
    ).astype(BF)

    def rotated(raw, head):
        values = raw[:, head_columns(head)]
        turned = jnp.dot(values, swap, preferred_element_type=F32)
        return (values.astype(F32) * cosines[...] + turned * sines[...]).astype(BF)

    load_q.wait()
    load_k.wait()

    @pl.loop(0, GROUP)
    def _(i):
        for core in (0, 1):
            head = GROUP * core + i
            q_rot[head] = rotated(q_raw, head)
            k_rot[head] = rotated(k_raw, head)
        send_rotated(i)
        local_rotated(i, True)

    send_own(1)

    send(residual.at[0, :, partner], res_other, res_sem.at[0], res_sem.at[1], (p, t, 1 - g))
    width = 2 * HALF
    starts = (
        (2 * (1 - t) + g) * width,
        (2 * (1 - t) + 1 - g) * width + HALF,
        (2 * t + g) * width,
        (2 * t + g) * width + HALF,
    )
    loads = [
        pltpu.make_async_copy(
            weight.at[:, pl.ds(pl.multiple_of(start, HEAD_DIM), HALF)], w_tiles.at[k], load_sem.at[2 + k]
        )
        for k, start in enumerate(starts)
    ]
    loads.append(pltpu.make_async_copy(residual.at[0, :, mine], res_own, load_sem.at[6]))
    loads.append(
        pltpu.make_async_copy(
            gate_table.at[:, pl.ds(pl.multiple_of((2 * t + g) * width, HEAD_DIM), width)], gate_rows, load_sem.at[7]
        )
    )
    for copy in loads:
        copy.start()

    def attend(i, b):
        start = ROWS * (1 - 2 // (1 + b) + 3 * (1 // (1 + b)))
        span = pl.ds(pl.multiple_of(start, ROWS), KEYS)
        scores = lax.dot_general(
            qb[i, block_rows(b), :], kb[i, span, :], (((1,), (1,)), ((), ())), preferred_element_type=F32
        )
        top = jnp.max(scores, axis=1, keepdims=True) * SCORE_SCALE
        high = top.astype(BF).astype(F32)
        low = (top - high).astype(BF).astype(F32)
        expo = jnp.exp2(scores * SCORE_SCALE - (high + low))
        total = jnp.sum(expo, axis=1, keepdims=True)
        summed = jnp.dot(expo.astype(BF), vb[i, span, :], preferred_element_type=F32)
        o_send[i, b, 0:ROWS, :] = summed.astype(BF)
        total_high = total.astype(BF).astype(F32)
        notes = jnp.zeros((NOTE, HEAD_DIM), F32)
        note_row = lax.broadcasted_iota(jnp.int32, (NOTE, HEAD_DIM), 0)
        for k, column in enumerate((high, low, total_high, total - total_high)):
            for part, (first, last) in enumerate(((0, HEAD_DIM), (HEAD_DIM, ROWS))):
                line = jnp.sum(jnp.where(same_lane(last - first), column[first:last], 0.0), axis=0, keepdims=True)
                notes = jnp.where(note_row == 4 * part + k, line, notes)
        o_send[i, b, ROWS:, :] = notes.astype(BF)

        block, core = b // 2, b % 2

        @pl.when(b == c)
        def _():
            pltpu.make_async_copy(
                o_send.at[i, b], o_recv.at[GROUP * c + i, 0], o_recv_sem.at[GROUP * c + i, 0]
            ).start()

        @pl.when(b != c)
        def _():
            place = (RING - block) % RING
            send(
                o_send.at[i, b],
                o_recv.at[GROUP * c + i, place],
                o_sem.at[i, b],
                o_recv_sem.at[GROUP * c + i, place],
                at(0, block, core),
            )

    def merge(head):
        for j in range(RING):
            await_bytes(o_recv.at[head, j], o_recv_sem.at[head, j])
        notes = [o_recv[head, j, ROWS:, :].astype(F32) for j in range(RING)]
        for part, (first, last) in enumerate(((0, HEAD_DIM), (HEAD_DIM, ROWS))):
            tops = [n[4 * part : 4 * part + 1] + n[4 * part + 1 : 4 * part + 2] for n in notes]
            totals = [n[4 * part + 2 : 4 * part + 3] + n[4 * part + 3 : 4 * part + 4] for n in notes]
            top = jnp.maximum(jnp.maximum(tops[0], tops[1]), jnp.maximum(tops[2], tops[3]))
            fades = [jnp.exp2(one - top) for one in tops]
            whole = fades[0] * totals[0] + fades[1] * totals[1] + fades[2] * totals[2] + fades[3] * totals[3]
            result = jnp.zeros((last - first, HEAD_DIM), F32)
            for j in range(RING):
                column = jnp.sum(
                    jnp.where(same_lane(last - first), fades[j] / whole, 0.0), axis=1, keepdims=True
                )
                result = result + o_recv[head, j, first:last, :].astype(F32) * column
            attn[head, first:last, :] = result.astype(BF)
        send(attn.at[head], attn_other.at[head], guide_send.at[head], guide_recv.at[head], (p, t, 1 - g))

    forward(0)
    send_own(2)

    @pl.loop(0, GROUP)
    def _(i):
        arrived(i)

        @pl.loop(0, 8)
        def _(n):
            @pl.when((n == 4) & (i < GROUP - 1))
            def _():
                forward(i + 1)

            @pl.when((n == 4) & (i < GROUP - 3))
            def _():
                send_own(i + 3)

            @pl.when((n == 6) & (i > 0))
            def _():
                merge(i - 1)
                merge(GROUP + i - 1)

            attend(i, (n + 4) % 8)

    merge(GROUP - 1)
    merge(2 * GROUP - 1)

    own_share = (GUIDE_SCALE - (2 * GUIDE_SCALE - 1) * g).astype(F32)
    other_share = (1.0 - GUIDE_SCALE + (2 * GUIDE_SCALE - 1) * g).astype(F32)

    @pl.loop(0, HEADS)
    def _(head):
        await_bytes(attn_other.at[head], guide_recv.at[head])
        both = own_share * attn[head].astype(F32) + other_share * attn_other[head].astype(F32)
        combined[:, head_columns(head)] = both.astype(BF)

    for copy in loads:
        copy.wait()

    neighbours = ((p, 1 - t, g), (p, 1 - t, 1 - g))
    for k in (0, 1):
        part_send[k] = jnp.dot(combined[...], w_tiles[k], preferred_element_type=F32).astype(BF)
        send(part_send.at[k], part_recv.at[k], part_send_sem.at[k], part_recv_sem.at[k], neighbours[k])
    for k in (0, 1):
        part_own[k] = jnp.dot(combined[...], w_tiles[2 + k], preferred_element_type=F32)
    await_bytes(res_other, res_sem.at[1])
    steps = lax.broadcasted_iota(jnp.int32, gate_rows.shape, 0)
    gate = jnp.sum(jnp.where(steps == timestep[0], gate_rows[...], 0.0), axis=0, keepdims=True)
    for k in (0, 1):
        columns = pl.ds(k * HALF, HALF)
        await_bytes(part_recv.at[k], part_recv_sem.at[k])
        base = own_share * res_own[:, columns].astype(F32) + other_share * res_other[:, columns].astype(F32)
        proj = part_own[k] + part_recv[k].astype(F32)
        out[:, columns] = (base + gate[:, k * HALF : (k + 1) * HALF] * proj).astype(BF)

    @pl.loop(0, GROUP)
    def _(i):
        for k in range(8):
            await_bytes(kb.at[i, block_rows(0), :], kv_sem.at[i, k])
        for k in range(4):
            await_bytes(q_rot.at[i], q_sem.at[i, k])
        await_bytes(kb.at[i, block_rows(2, 2), :], far_sem.at[i, 0])
        await_bytes(vb.at[i, block_rows(4, 2), :], far_sem.at[i, 1])
        await_bytes(qb.at[i, block_rows(6), :], far_sem.at[i, 2])
        await_bytes(qb.at[i, block_rows(3), :], far_sem.at[i, 3])
        for k in range(5):
            await_bytes(q_rot.at[i], sib_sem.at[i, k])

        @pl.loop(0, 8)
        def _(b):
            @pl.when(b != c)
            def _():
                await_bytes(o_send.at[i, b], o_sem.at[i, b])

    @pl.loop(0, HEADS)
    def _(head):
        await_bytes(attn.at[head], guide_send.at[head])

    await_bytes(res_other, res_sem.at[0])
    for k in (0, 1):
        await_bytes(part_send.at[k], part_send_sem.at[k])


def per_device(
    fresh_q, fresh_k, fresh_v, stale_k, stale_v, positions, residual, out_weight, gate_table, timestep
):
    width = 2 * HALF
    steps = gate_table.shape[0]
    in_hbm = pl.BlockSpec(memory_space=pl.ANY)
    in_vmem = pl.BlockSpec(memory_space=pltpu.VMEM)
    dma = pltpu.SemaphoreType.DMA
    return pl.pallas_call(
        kernel,
        out_shape=jax.ShapeDtypeStruct((ROWS, width), BF),
        in_specs=[in_hbm] * 8 + [in_vmem, in_vmem, pl.BlockSpec(memory_space=pltpu.SMEM)],
        out_specs=in_vmem,
        scratch_shapes=[
            pltpu.VMEM((GROUP, 10 * ROWS, HEAD_DIM), BF),
            pltpu.VMEM((GROUP, 10 * ROWS, HEAD_DIM), BF),
            pltpu.VMEM((GROUP, 8 * ROWS, HEAD_DIM), BF),
            pltpu.VMEM((ROWS, width), BF),
            pltpu.VMEM((ROWS, width), BF),
            pltpu.VMEM((HEADS, ROWS, HEAD_DIM), BF),
            pltpu.VMEM((HEADS, ROWS, HEAD_DIM), BF),
            pltpu.VMEM((GROUP, 8, ROWS + NOTE, HEAD_DIM), BF),
            pltpu.VMEM((HEADS, RING, ROWS + NOTE, HEAD_DIM), BF),
            pltpu.VMEM((HEADS, ROWS, HEAD_DIM), BF),
            pltpu.VMEM((HEADS, ROWS, HEAD_DIM), BF),
            pltpu.VMEM((ROWS, width), BF),
            pltpu.VMEM((4, width, HALF), BF),
            pltpu.VMEM((2, ROWS, HALF), BF),
            pltpu.VMEM((2, ROWS, HALF), BF),
            pltpu.VMEM((2, ROWS, HALF), F32),
            pltpu.VMEM((ROWS, width), BF),
            pltpu.VMEM((ROWS, width), BF),
            pltpu.VMEM((steps, width), F32),
            pltpu.VMEM((ROWS, HEAD_DIM), F32),
            pltpu.VMEM((ROWS, HEAD_DIM), F32),
            dma((KINDS * GROUP,)),
            dma((HEADS, RING)),
            dma((GROUP, 8)),
            dma((GROUP, 4)),
            dma((GROUP, 4)),
            dma((GROUP, 5)),
            dma((GROUP, 5)),
            dma((GROUP, 8)),
            dma((HEADS,)),
            dma((HEADS,)),
            dma((2,)),
            dma((2,)),
            dma((2,)),
            dma((8,)),
        ],
        compiler_params=pltpu.CompilerParams(
            collective_id=0, has_side_effects=True, vmem_limit_bytes=56 * 1024 * 1024
        ),
        cost_estimate=pl.CostEstimate(flops=8_000_000_000, bytes_accessed=12_000_000, transcendentals=12_000_000),
    )(
        fresh_q, fresh_k, fresh_v, stale_k, stale_v, residual, out_weight, gate_table,
        jnp.asarray(frequencies()), positions, timestep,
    )


def solution(mesh):
    in_specs = (
        P("guide", "patch", "tensor"),
        P("guide", "patch", "tensor"),
        P("guide", "patch", "tensor"),
        P("guide", "patch", "tensor"),
        P("guide", "patch", "tensor"),
        P(None, "patch"),
        P("guide", "patch", "tensor"),
        P("tensor", None),
        P(),
        P(),
    )
    out_specs = P("patch", ("tensor", "guide"))
    return jax.shard_map(per_device, mesh=mesh, in_specs=in_specs, out_specs=out_specs, check_vma=False)
```

time: 283 us -> 87.6 us (0.31)
  waiting for transfers between devices: 171 us -> 0 us
  Pallas kernels: 0 us -> 84.5 us
  matrix products: 57.7 us -> 0 us
  blocking collectives: 18.3 us -> 0 us
  between operations: 14 us -> 0.66 us
  other arithmetic: 12.1 us -> 0 us
  local copies, waits for them, and re-layouts: 8.85 us -> 1.84 us
    all_gather x2 -> x0, waiting for transfers between devices: 138 us -> none  [the longest x1 71.1 us: per_device(): lax.all_gather(stale_v[0], 'patch', axis=0, tiled=True)]
    pallas_call x0 -> x1, Pallas kernels: none -> 84.5 us  [per_device(): pl.pallas_call(kernel, out_shape=jax.ShapeDtypeStruct((ROWS, width), BF),...]
    dot_general x24 -> x0, matrix products: 57.7 us -> none  [the longest x10 23.8 us: one_head(): jnp.dot(expo.astype(jnp.bfloat16), value_head, preferred_element_type=jnp...]
    reduce_scatter x1 -> x0, waiting for transfers between devices: 31.4 us -> none  [per_device(): lax.psum_scatter(partial_value.astype(jnp.bfloat16), 'tensor', scatter_di...]
    all_to_all x1 -> x0, blocking collectives: 18.3 us -> none  [per_device(): lax.all_to_all(hidden.reshape(tok_rows, 2, half_cols // 2).astype(jnp.bfl...]
    reduce_sum x10 -> x0, other arithmetic: 7.94 us -> none  [one_head(): total_new = total_old * fade + jnp.sum(expo, axis=1)]
    dynamic_update_slice x22 -> x0, local copies, waits for them, and re-layouts: 3.52 us -> none  [the longest x1 1.85 us: per_device(): lax.dynamic_update_slice_in_dim(values_all, values_own, own_start, 0)]
    convert_element_type x4 -> x0, other arithmetic: 3.2 us -> none  [the longest x1 1.49 us: per_device(): hidden.reshape(tok_rows, 2, half_cols // 2).astype(jnp.bfloat16)]
  transfers between devices with their start and end apart: 3 -> 0, of which waited for: 3 -> 0; matrix products, arithmetic and copies ran while one was open for 3% -> 0% of each run, Pallas kernels for 0% -> 0%
where the time goes in v1:
time: 87.6 us; the launch traced here: 87 us
  Pallas kernels  84.5 us (96%)
  local copies, waits for them, and re-layouts  1.84 us (2%)
    pallas_call x1, Pallas kernels, per_device(): pl.pallas_call(kernel, out_shape=jax.ShapeDtypeStruct((ROWS, width), BF),...  84.5 us
    unnamed x1, local copies, waits for them, and re-layouts  1.84 us

profile of v1, /device:TPU:0, one launch (start us, length us, event | category | flops | bytes accessed | tf_op | source)
XLA Modules:
  0.0 87.0 jit_solution(12471841195148006020)
XLA Ops:
  0.7 84.5 %shard_map.109 = bf16[192,1280]{1,0:T(8,128)(2,1)} custom-call(bf16[1,192,1280]{2,1,0:T(8,128)(2,1)} %fresh_q.1, bf16[1,192,1280]{2,1,0:T(8,128)(2,1)} %fresh_k.1, bf16[1,192,1280]{2,1,0:T(8,128)(2,1)} %fresh_v.1, bf16[1,192,1280]{2,1,0:T(8,128)(2,1)} %stale_k.1, bf16[1,192,1280]{2,1,0:T(8,128)(2,1)} %stale_v.1, bf16[1,192,2560]{2,1,0:T(8,128)(2,1)} %residual.1, ...), custom_call_target="tpu_custom_call" | custom-call | flops 8000000000 | bytes 12000000 | tf_op jit(solution)/shard_map/pallas_call | solution.py:406
  85.1 1.8 %copy.14 = bf16[192,1280]{1,0:T(8,128)(2,1)} copy(bf16[192,1280]{1,0:T(8,128)(2,1)} %shard_map.109) | data formatting | bytes 983040

commit v2 on v1

--- a/solution.py
+++ b/solution.py
@@ -115,8 +115,8 @@
         for copy in copies:
             copy.start() if start else copy.wait()
 
-    def send_own(i):
-        for core in (0, 1):
+    def send_own(i, *cores):
+        for core in cores or (0, 1):
             columns = head_columns(GROUP * core + i)
             for tensor, (source, buf) in enumerate(((stale_k, kb), (stale_v, vb))):
                 for way, (dx, slot, kind) in enumerate(((1, 2, 2 * tensor), (3, 4, 2 * tensor + 1))):
@@ -180,13 +180,9 @@
         await_bytes(vb.at[i, block_rows(6, 2), :], got(V_FAR, i))
         await_bytes(qb.at[i, block_rows(4, 2), :], got(Q_FAR, i))
 
-    pl.semaphore_wait(barrier, len(peers))
-    send_own(0)
-
     @pl.loop(0, GROUP)
     def _(i):
         local_stale(i, True)
-        send_sibling_stale(i)
 
     res_columns = residual.shape[2] // 2
     mine = pl.ds(pl.multiple_of(g * res_columns, HEAD_DIM), res_columns)
@@ -224,10 +220,20 @@
             head = GROUP * core + i
             q_rot[head] = rotated(q_raw, head)
             k_rot[head] = rotated(k_raw, head)
+        local_rotated(i, True)
+
+    pl.semaphore_wait(barrier, len(peers))
+
+    @pl.loop(0, GROUP)
+    def _(i):
+        @pl.when(i == 0)
+        def _():
+            send_own(0)
+
         send_rotated(i)
-        local_rotated(i, True)
-
-    send_own(1)
+        send_sibling_stale(i)
+
+    send_own(1, 0)
 
     send(residual.at[0, :, partner], res_other, res_sem.at[0], res_sem.at[1], (p, t, 1 - g))
     width = 2 * HALF
@@ -274,6 +280,7 @@
                 notes = jnp.where(note_row == 4 * part + k, line, notes)
         o_send[i, b, ROWS:, :] = notes.astype(BF)
 
+    def send_back(i, b):
         block, core = b // 2, b % 2
 
         @pl.when(b == c)
@@ -313,28 +320,33 @@
         send(attn.at[head], attn_other.at[head], guide_send.at[head], guide_recv.at[head], (p, t, 1 - g))
 
     forward(0)
+    send_own(1, 1)
     send_own(2)
 
     @pl.loop(0, GROUP)
     def _(i):
+        @pl.when(i < GROUP - 1)
+        def _():
+            forward(i + 1)
+
+        @pl.when(i < GROUP - 3)
+        def _():
+            send_own(i + 3)
+
         arrived(i)
 
-        @pl.loop(0, 8)
+        @pl.loop(0, RING)
         def _(n):
-            @pl.when((n == 4) & (i < GROUP - 1))
-            def _():
-                forward(i + 1)
-
-            @pl.when((n == 4) & (i < GROUP - 3))
-            def _():
-                send_own(i + 3)
-
-            @pl.when((n == 6) & (i > 0))
+            @pl.when((n == 3) & (i > 0))
             def _():
                 merge(i - 1)
                 merge(GROUP + i - 1)
 
-            attend(i, (n + 4) % 8)
+            block = (n + 2) % RING
+            attend(i, 2 * block)
+            attend(i, 2 * block + 1)
+            send_back(i, 2 * block)
+            send_back(i, 2 * block + 1)
 
     merge(GROUP - 1)
     merge(2 * GROUP - 1)

time: 87.6 us -> 78.5 us (0.90)
  Pallas kernels: 84.5 us -> 75.1 us
    pallas_call x1, Pallas kernels: 84.5 us -> 75.1 us  [per_device(): pl.pallas_call(kernel, out_shape=jax.ShapeDtypeStruct((ROWS, width), BF),...]
where the time goes in v2:
time: 78.5 us; the launch traced here: 77.6 us
  Pallas kernels  75.1 us (96%)
  local copies, waits for them, and re-layouts  1.84 us (2%)
    pallas_call x1, Pallas kernels, per_device(): pl.pallas_call(kernel, out_shape=jax.ShapeDtypeStruct((ROWS, width), BF),...  75.1 us
    unnamed x1, local copies, waits for them, and re-layouts  1.84 us

profile of v2, /device:TPU:0, one launch (start us, length us, event | category | flops | bytes accessed | tf_op | source)
XLA Modules:
  0.0 77.6 jit_solution(15043890486963135746)
XLA Ops:
  0.7 75.1 %shard_map.109 = bf16[192,1280]{1,0:T(8,128)(2,1)} custom-call(bf16[1,192,1280]{2,1,0:T(8,128)(2,1)} %fresh_q.1, bf16[1,192,1280]{2,1,0:T(8,128)(2,1)} %fresh_k.1, bf16[1,192,1280]{2,1,0:T(8,128)(2,1)} %fresh_v.1, bf16[1,192,1280]{2,1,0:T(8,128)(2,1)} %stale_k.1, bf16[1,192,1280]{2,1,0:T(8,128)(2,1)} %stale_v.1, bf16[1,192,2560]{2,1,0:T(8,128)(2,1)} %residual.1, ...), custom_call_target="tpu_custom_call" | custom-call | flops 8000000000 | bytes 12000000 | tf_op jit(solution)/shard_map/pallas_call | solution.py:418
  75.8 1.8 %copy.14 = bf16[192,1280]{1,0:T(8,128)(2,1)} copy(bf16[192,1280]{1,0:T(8,128)(2,1)} %shard_map.109) | data formatting | bytes 983040

commit v3 on v2

--- a/solution.py
+++ b/solution.py
@@ -59,7 +59,7 @@
 def kernel(
     fresh_q, fresh_k, fresh_v, stale_k, stale_v, residual, weight, gate_table, freqs, positions, timestep,
     out,
-    kb, vb, qb, q_raw, k_raw, q_rot, k_rot, o_send, o_recv, attn, attn_other, combined, w_tiles, part_send, part_recv,
+    kb, vb, qb, scores_a, scores_b, weights_a, weights_b, q_raw, k_raw, q_rot, k_rot, o_send, o_recv, attn, attn_other, combined, w_tiles, part_send, part_recv,
     part_own, res_own, res_other, gate_rows, cosines, sines,
     recv, o_recv_sem, kv_sem, q_sem, far_sem, sib_sem, local_sem, o_sem, guide_send, guide_recv, part_send_sem,
     part_recv_sem, res_sem, load_sem,
@@ -140,6 +140,8 @@
         device = at(0, 0, sib)
         send(q_rot.at[head], qb.at[i, block_rows(c), :], sib_sem.at[i, 3], got(SIB_Q, i), device)
         send(k_rot.at[head], kb.at[i, block_rows(fresh_slot), :], sib_sem.at[i, 4], got(SIB_FK, i), device)
+
+    def send_queries(i):
         for core in (0, 1):
             for way, (dy, block, kind) in enumerate(((1, 6, Q_LEFT), (3, 2, Q_RIGHT))):
                 send(
@@ -150,7 +152,13 @@
                     at(0, dy, core),
                 )
 
-    def forward(i):
+    def forward_queries(i):
+        await_bytes(qb.at[i, block_rows(6, 2), :], got(Q_LEFT, i))
+        send(qb.at[i, block_rows(6), :], qb.at[i, block_rows(4), :], far_sem.at[i, 2], got(Q_FAR, i), at(0, 1, c))
+        await_bytes(qb.at[i, block_rows(2, 2), :], got(Q_RIGHT, i))
+        send(qb.at[i, block_rows(3), :], qb.at[i, block_rows(5), :], far_sem.at[i, 3], got(Q_FAR, i), at(0, 3, c))
+
+    def forward_keys(i):
         await_bytes(kb.at[i, block_rows(2, 2), :], got(K_LEFT, i))
         send(
             kb.at[i, block_rows(2, 2), :], kb.at[i, block_rows(6, 2), :], far_sem.at[i, 0], got(K_FAR, i), at(1, 0, c)
@@ -159,10 +167,6 @@
         send(
             vb.at[i, block_rows(4, 2), :], vb.at[i, block_rows(6, 2), :], far_sem.at[i, 1], got(V_FAR, i), at(3, 0, c)
         )
-        await_bytes(qb.at[i, block_rows(6, 2), :], got(Q_LEFT, i))
-        send(qb.at[i, block_rows(6), :], qb.at[i, block_rows(4), :], far_sem.at[i, 2], got(Q_FAR, i), at(0, 1, c))
-        await_bytes(qb.at[i, block_rows(2, 2), :], got(Q_RIGHT, i))
-        send(qb.at[i, block_rows(3), :], qb.at[i, block_rows(5), :], far_sem.at[i, 3], got(Q_FAR, i), at(0, 3, c))
 
     def arrived(i):
         local_stale(i, False)
@@ -224,16 +228,16 @@
 
     pl.semaphore_wait(barrier, len(peers))
 
+    send_own(0)
+    send_queries(0)
+
     @pl.loop(0, GROUP)
     def _(i):
-        @pl.when(i == 0)
-        def _():
-            send_own(0)
-
+        send_sibling_stale(i)
         send_rotated(i)
-        send_sibling_stale(i)
 
     send_own(1, 0)
+    send_queries(1)
 
     send(residual.at[0, :, partner], res_other, res_sem.at[0], res_sem.at[1], (p, t, 1 - g))
     width = 2 * HALF
@@ -258,39 +262,50 @@
     for copy in loads:
         copy.start()
 
-    def attend(i, b):
-        start = ROWS * (1 - 2 // (1 + b) + 3 * (1 // (1 + b)))
-        span = pl.ds(pl.multiple_of(start, ROWS), KEYS)
-        scores = lax.dot_general(
-            qb[i, block_rows(b), :], kb[i, span, :], (((1,), (1,)), ((), ())), preferred_element_type=F32
-        )
-        top = jnp.max(scores, axis=1, keepdims=True) * SCORE_SCALE
-        high = top.astype(BF).astype(F32)
-        low = (top - high).astype(BF).astype(F32)
-        expo = jnp.exp2(scores * SCORE_SCALE - (high + low))
-        total = jnp.sum(expo, axis=1, keepdims=True)
-        summed = jnp.dot(expo.astype(BF), vb[i, span, :], preferred_element_type=F32)
-        o_send[i, b, 0:ROWS, :] = summed.astype(BF)
-        total_high = total.astype(BF).astype(F32)
-        notes = jnp.zeros((NOTE, HEAD_DIM), F32)
-        note_row = lax.broadcasted_iota(jnp.int32, (NOTE, HEAD_DIM), 0)
-        for k, column in enumerate((high, low, total_high, total - total_high)):
+    def pieces(chip):
+        if chip:
+            return [(0, 2 * ROWS, ROWS)]
+        return [(0, ROWS, 2 * ROWS), (ROWS, 2 * ROWS, 0)]
+
+    def score(i, chip, scores):
+        for first, last, keys in pieces(chip):
+            scores[first:last, :] = lax.dot_general(
+                qb[i, 2 * chip * ROWS + first : 2 * chip * ROWS + last, :],
+                kb[i, keys : keys + KEYS, :],
+                (((1,), (1,)), ((), ())),
+                preferred_element_type=F32,
+            )
+
+    def soften(i, chip, scores, weights):
+        for half in (0, 1):
+            rows = slice(half * ROWS, (half + 1) * ROWS)
+            top = jnp.max(scores[rows, :], axis=1, keepdims=True) * SCORE_SCALE
+            expo = jnp.exp2(scores[rows, :] * SCORE_SCALE - top)
+            total = jnp.sum(expo, axis=1, keepdims=True)
+            weights[rows, :] = expo.astype(BF)
+            notes = jnp.zeros((NOTE, HEAD_DIM), F32)
+            note_row = lax.broadcasted_iota(jnp.int32, (NOTE, HEAD_DIM), 0)
             for part, (first, last) in enumerate(((0, HEAD_DIM), (HEAD_DIM, ROWS))):
-                line = jnp.sum(jnp.where(same_lane(last - first), column[first:last], 0.0), axis=0, keepdims=True)
-                notes = jnp.where(note_row == 4 * part + k, line, notes)
-        o_send[i, b, ROWS:, :] = notes.astype(BF)
+                for k, (column, count) in enumerate(((top, 3), (total, 2))):
+                    rest = jnp.sum(jnp.where(same_lane(last - first), column[first:last], 0.0), axis=0, keepdims=True)
+                    for piece in range(count):
+                        line = rest.astype(BF).astype(F32)
+                        rest = rest - line
+                        notes = jnp.where(note_row == 8 * part + 3 * k + piece, line, notes)
+            o_send[i, 2 * chip + half, ROWS:, :] = notes.astype(BF)
+
+    def weigh(i, chip, weights):
+        for first, last, keys in pieces(chip):
+            summed = jnp.dot(
+                weights[first:last, :], vb[i, keys : keys + KEYS, :], preferred_element_type=F32
+            ).astype(BF)
+            for row in range(first, last, ROWS):
+                o_send[i, 2 * chip + row // ROWS, 0:ROWS, :] = summed[row - first : row - first + ROWS]
 
     def send_back(i, b):
         block, core = b // 2, b % 2
 
-        @pl.when(b == c)
-        def _():
-            pltpu.make_async_copy(
-                o_send.at[i, b], o_recv.at[GROUP * c + i, 0], o_recv_sem.at[GROUP * c + i, 0]
-            ).start()
-
-        @pl.when(b != c)
-        def _():
+        def away():
             place = (RING - block) % RING
             send(
                 o_send.at[i, b],
@@ -300,13 +315,25 @@
                 at(0, block, core),
             )
 
+        if block:
+            away()
+        else:
+            pl.when(core != c)(away)
+
+            @pl.when(core == c)
+            def _():
+                pltpu.make_async_copy(
+                    o_send.at[i, b], o_recv.at[GROUP * c + i, 0], o_recv_sem.at[GROUP * c + i, 0]
+                ).start()
+
     def merge(head):
         for j in range(RING):
             await_bytes(o_recv.at[head, j], o_recv_sem.at[head, j])
         notes = [o_recv[head, j, ROWS:, :].astype(F32) for j in range(RING)]
         for part, (first, last) in enumerate(((0, HEAD_DIM), (HEAD_DIM, ROWS))):
-            tops = [n[4 * part : 4 * part + 1] + n[4 * part + 1 : 4 * part + 2] for n in notes]
-            totals = [n[4 * part + 2 : 4 * part + 3] + n[4 * part + 3 : 4 * part + 4] for n in notes]
+            lines = [[n[8 * part + k : 8 * part + k + 1] for k in range(5)] for n in notes]
+            tops = [line[0] + line[1] + line[2] for line in lines]
+            totals = [line[3] + line[4] for line in lines]
             top = jnp.maximum(jnp.maximum(tops[0], tops[1]), jnp.maximum(tops[2], tops[3]))
             fades = [jnp.exp2(one - top) for one in tops]
             whole = fades[0] * totals[0] + fades[1] * totals[1] + fades[2] * totals[2] + fades[3] * totals[3]
@@ -319,7 +346,9 @@
             attn[head, first:last, :] = result.astype(BF)
         send(attn.at[head], attn_other.at[head], guide_send.at[head], guide_recv.at[head], (p, t, 1 - g))
 
-    forward(0)
+    forward_queries(0)
+    send_queries(2)
+    forward_keys(0)
     send_own(1, 1)
     send_own(2)
 
@@ -327,26 +356,34 @@
     def _(i):
         @pl.when(i < GROUP - 1)
         def _():
-            forward(i + 1)
+            forward_queries(i + 1)
+            forward_keys(i + 1)
 
         @pl.when(i < GROUP - 3)
         def _():
+            send_queries(i + 3)
             send_own(i + 3)
 
         arrived(i)
 
-        @pl.loop(0, RING)
-        def _(n):
-            @pl.when((n == 3) & (i > 0))
-            def _():
-                merge(i - 1)
-                merge(GROUP + i - 1)
-
-            block = (n + 2) % RING
-            attend(i, 2 * block)
-            attend(i, 2 * block + 1)
-            send_back(i, 2 * block)
-            send_back(i, 2 * block + 1)
+        order = (2, 3, 1, 0)
+        scores = (scores_a, scores_b)
+        weights = (weights_a, weights_b)
+        for n in range(len(order) + 2):
+            if n >= 2:
+                weigh(i, order[n - 2], weights[n % 2])
+            if n < len(order):
+                score(i, order[n], scores[n % 2])
+            if 1 <= n <= len(order):
+                soften(i, order[n - 1], scores[(n - 1) % 2], weights[(n - 1) % 2])
+            if n >= 2:
+                send_back(i, 2 * order[n - 2])
+                send_back(i, 2 * order[n - 2] + 1)
+
+        @pl.when(i > 0)
+        def _():
+            merge(i - 1)
+            merge(GROUP + i - 1)
 
     merge(GROUP - 1)
     merge(2 * GROUP - 1)
@@ -424,6 +461,10 @@
             pltpu.VMEM((GROUP, 10 * ROWS, HEAD_DIM), BF),
             pltpu.VMEM((GROUP, 10 * ROWS, HEAD_DIM), BF),
             pltpu.VMEM((GROUP, 8 * ROWS, HEAD_DIM), BF),
+            pltpu.VMEM((2 * ROWS, KEYS), F32),
+            pltpu.VMEM((2 * ROWS, KEYS), F32),
+            pltpu.VMEM((2 * ROWS, KEYS), BF),
+            pltpu.VMEM((2 * ROWS, KEYS), BF),
             pltpu.VMEM((ROWS, width), BF),
             pltpu.VMEM((ROWS, width), BF),
             pltpu.VMEM((HEADS, ROWS, HEAD_DIM), BF),

time: 78.5 us -> 75 us (0.955)
  Pallas kernels: 75.1 us -> 71.7 us
    pallas_call x1, Pallas kernels: 75.1 us -> 71.7 us  [per_device(): pl.pallas_call(kernel, out_shape=jax.ShapeDtypeStruct((ROWS, width), BF),...]
where the time goes in v3:
time: 75 us; the launch traced here: 74.2 us
  Pallas kernels  71.7 us (96%)
  local copies, waits for them, and re-layouts  1.84 us (2%)
    pallas_call x1, Pallas kernels, per_device(): pl.pallas_call(kernel, out_shape=jax.ShapeDtypeStruct((ROWS, width), BF),...  71.7 us
    unnamed x1, local copies, waits for them, and re-layouts  1.84 us

profile of v3, /device:TPU:0, one launch (start us, length us, event | category | flops | bytes accessed | tf_op | source)
XLA Modules:
  0.0 74.2 jit_solution(6364980654326809212)
XLA Ops:
  0.7 71.7 %shard_map.109 = bf16[192,1280]{1,0:T(8,128)(2,1)} custom-call(bf16[1,192,1280]{2,1,0:T(8,128)(2,1)} %fresh_q.1, bf16[1,192,1280]{2,1,0:T(8,128)(2,1)} %fresh_k.1, bf16[1,192,1280]{2,1,0:T(8,128)(2,1)} %fresh_v.1, bf16[1,192,1280]{2,1,0:T(8,128)(2,1)} %stale_k.1, bf16[1,192,1280]{2,1,0:T(8,128)(2,1)} %stale_v.1, bf16[1,192,2560]{2,1,0:T(8,128)(2,1)} %residual.1, ...), custom_call_target="tpu_custom_call" | custom-call | flops 8000000000 | bytes 12000000 | tf_op jit(solution)/shard_map/pallas_call | solution.py:455
  72.4 1.8 %copy.14 = bf16[192,1280]{1,0:T(8,128)(2,1)} copy(bf16[192,1280]{1,0:T(8,128)(2,1)} %shard_map.109) | data formatting | bytes 983040

commit v4 on v3

--- a/solution.py
+++ b/solution.py
@@ -60,7 +60,7 @@
     fresh_q, fresh_k, fresh_v, stale_k, stale_v, residual, weight, gate_table, freqs, positions, timestep,
     out,
     kb, vb, qb, scores_a, scores_b, weights_a, weights_b, q_raw, k_raw, q_rot, k_rot, o_send, o_recv, attn, attn_other, combined, w_tiles, part_send, part_recv,
-    part_own, res_own, res_other, gate_rows, cosines, sines,
+    part, base, res_own, res_other, gate_rows, cosines, sines,
     recv, o_recv_sem, kv_sem, q_sem, far_sem, sib_sem, local_sem, o_sem, guide_send, guide_recv, part_send_sem,
     part_recv_sem, res_sem, load_sem,
 ):
@@ -106,14 +106,11 @@
         for copy in copies:
             copy.start() if start else copy.wait()
 
-    def local_rotated(i, start):
-        head = GROUP * c + i
-        copies = (
-            pltpu.make_async_copy(k_rot.at[head], kb.at[i, block_rows(fresh_slot), :], local_sem.at[i, 3]),
-            pltpu.make_async_copy(q_rot.at[head], qb.at[i, block_rows(c), :], local_sem.at[i, 4]),
-        )
-        for copy in copies:
-            copy.start() if start else copy.wait()
+    own_heads = pl.ds(GROUP * c, GROUP)
+    local_rotated = (
+        pltpu.make_async_copy(k_rot.at[own_heads], kb.at[:, block_rows(fresh_slot), :], load_sem.at[8]),
+        pltpu.make_async_copy(q_rot.at[own_heads], qb.at[:, block_rows(c), :], load_sem.at[9]),
+    )
 
     def send_own(i, *cores):
         for core in cores or (0, 1):
@@ -135,11 +132,11 @@
         send(stale_v.at[0, :, columns], vb.at[i, block_rows(own_slot), :], sib_sem.at[i, 1], got(SIB_V, i), device)
         send(fresh_v.at[0, :, columns], vb.at[i, block_rows(fresh_slot), :], sib_sem.at[i, 2], got(SIB_FV, i), device)
 
-    def send_rotated(i):
-        head = GROUP * sib + i
+    def send_rotated():
+        heads = pl.ds(GROUP * sib, GROUP)
         device = at(0, 0, sib)
-        send(q_rot.at[head], qb.at[i, block_rows(c), :], sib_sem.at[i, 3], got(SIB_Q, i), device)
-        send(k_rot.at[head], kb.at[i, block_rows(fresh_slot), :], sib_sem.at[i, 4], got(SIB_FK, i), device)
+        send(q_rot.at[heads], qb.at[:, block_rows(c), :], sib_sem.at[0, 3], got(SIB_Q, 0), device)
+        send(k_rot.at[heads], kb.at[:, block_rows(fresh_slot), :], sib_sem.at[0, 4], got(SIB_FK, 0), device)
 
     def send_queries(i):
         for core in (0, 1):
@@ -170,23 +167,24 @@
 
     def arrived(i):
         local_stale(i, False)
-        local_rotated(i, False)
         other = 8 - 7 * c
         other_fresh = 9 * c
         await_bytes(kb.at[i, block_rows(other), :], got(SIB_K, i))
         await_bytes(vb.at[i, block_rows(other), :], got(SIB_V, i))
-        await_bytes(kb.at[i, block_rows(other_fresh), :], got(SIB_FK, i))
         await_bytes(vb.at[i, block_rows(other_fresh), :], got(SIB_FV, i))
-        await_bytes(qb.at[i, block_rows(sib), :], got(SIB_Q, i))
+
+        @pl.when(i == 0)
+        def _():
+            for copy in local_rotated:
+                copy.wait()
+            await_bytes(kb.at[:, block_rows(other_fresh), :], got(SIB_FK, 0))
+            await_bytes(qb.at[:, block_rows(sib), :], got(SIB_Q, 0))
+
         await_bytes(kb.at[i, block_rows(4, 2), :], got(K_RIGHT, i))
         await_bytes(vb.at[i, block_rows(2, 2), :], got(V_LEFT, i))
         await_bytes(kb.at[i, block_rows(6, 2), :], got(K_FAR, i))
         await_bytes(vb.at[i, block_rows(6, 2), :], got(V_FAR, i))
         await_bytes(qb.at[i, block_rows(4, 2), :], got(Q_FAR, i))
-
-    @pl.loop(0, GROUP)
-    def _(i):
-        local_stale(i, True)
 
     res_columns = residual.shape[2] // 2
     mine = pl.ds(pl.multiple_of(g * res_columns, HEAD_DIM), res_columns)
@@ -224,20 +222,23 @@
             head = GROUP * core + i
             q_rot[head] = rotated(q_raw, head)
             k_rot[head] = rotated(k_raw, head)
-        local_rotated(i, True)
 
     pl.semaphore_wait(barrier, len(peers))
 
     send_own(0)
     send_queries(0)
-
-    @pl.loop(0, GROUP)
+    send_rotated()
+    send_sibling_stale(0)
+    local_stale(0, True)
+    for copy in local_rotated:
+        copy.start()
+    send_own(1, 0)
+    send_queries(1)
+
+    @pl.loop(1, GROUP)
     def _(i):
         send_sibling_stale(i)
-        send_rotated(i)
-
-    send_own(1, 0)
-    send_queries(1)
+        local_stale(i, True)
 
     send(residual.at[0, :, partner], res_other, res_sem.at[0], res_sem.at[1], (p, t, 1 - g))
     width = 2 * HALF
@@ -385,37 +386,6 @@
             merge(i - 1)
             merge(GROUP + i - 1)
 
-    merge(GROUP - 1)
-    merge(2 * GROUP - 1)
-
-    own_share = (GUIDE_SCALE - (2 * GUIDE_SCALE - 1) * g).astype(F32)
-    other_share = (1.0 - GUIDE_SCALE + (2 * GUIDE_SCALE - 1) * g).astype(F32)
-
-    @pl.loop(0, HEADS)
-    def _(head):
-        await_bytes(attn_other.at[head], guide_recv.at[head])
-        both = own_share * attn[head].astype(F32) + other_share * attn_other[head].astype(F32)
-        combined[:, head_columns(head)] = both.astype(BF)
-
-    for copy in loads:
-        copy.wait()
-
-    neighbours = ((p, 1 - t, g), (p, 1 - t, 1 - g))
-    for k in (0, 1):
-        part_send[k] = jnp.dot(combined[...], w_tiles[k], preferred_element_type=F32).astype(BF)
-        send(part_send.at[k], part_recv.at[k], part_send_sem.at[k], part_recv_sem.at[k], neighbours[k])
-    for k in (0, 1):
-        part_own[k] = jnp.dot(combined[...], w_tiles[2 + k], preferred_element_type=F32)
-    await_bytes(res_other, res_sem.at[1])
-    steps = lax.broadcasted_iota(jnp.int32, gate_rows.shape, 0)
-    gate = jnp.sum(jnp.where(steps == timestep[0], gate_rows[...], 0.0), axis=0, keepdims=True)
-    for k in (0, 1):
-        columns = pl.ds(k * HALF, HALF)
-        await_bytes(part_recv.at[k], part_recv_sem.at[k])
-        base = own_share * res_own[:, columns].astype(F32) + other_share * res_other[:, columns].astype(F32)
-        proj = part_own[k] + part_recv[k].astype(F32)
-        out[:, columns] = (base + gate[:, k * HALF : (k + 1) * HALF] * proj).astype(BF)
-
     @pl.loop(0, GROUP)
     def _(i):
         for k in range(8):
@@ -426,20 +396,73 @@
         await_bytes(vb.at[i, block_rows(4, 2), :], far_sem.at[i, 1])
         await_bytes(qb.at[i, block_rows(6), :], far_sem.at[i, 2])
         await_bytes(qb.at[i, block_rows(3), :], far_sem.at[i, 3])
-        for k in range(5):
+        for k in range(3):
             await_bytes(q_rot.at[i], sib_sem.at[i, k])
 
-        @pl.loop(0, 8)
-        def _(b):
+    for k in (3, 4):
+        await_bytes(q_rot.at[0:GROUP], sib_sem.at[0, k])
+    for copy in loads:
+        copy.wait()
+    await_bytes(res_other, res_sem.at[0])
+    await_bytes(res_other, res_sem.at[1])
+    own_share = (GUIDE_SCALE - (2 * GUIDE_SCALE - 1) * g).astype(F32)
+    other_share = (1.0 - GUIDE_SCALE + (2 * GUIDE_SCALE - 1) * g).astype(F32)
+    base[...] = own_share * res_own[...].astype(F32) + other_share * res_other[...].astype(F32)
+    steps = lax.broadcasted_iota(jnp.int32, gate_rows.shape, 0)
+    gate = jnp.sum(jnp.where(steps == timestep[0], gate_rows[...], 0.0), axis=0, keepdims=True)
+
+    merge(GROUP - 1)
+    merge(2 * GROUP - 1)
+
+    def combine(head):
+        await_bytes(attn_other.at[head], guide_recv.at[head])
+        both = own_share * attn[head].astype(F32) + other_share * attn_other[head].astype(F32)
+        combined[:, head_columns(head)] = both.astype(BF)
+
+    late = (slice((GROUP - 1) * HEAD_DIM, GROUP * HEAD_DIM), slice((HEADS - 1) * HEAD_DIM, HEADS * HEAD_DIM))
+    early = (slice(0, (GROUP - 1) * HEAD_DIM), slice(GROUP * HEAD_DIM, (HEADS - 1) * HEAD_DIM))
+
+    def project(k, spans):
+        first, second = (
+            jnp.dot(combined[:, span], w_tiles[k, span, :], preferred_element_type=F32) for span in spans
+        )
+        return first + second
+
+    @pl.loop(0, GROUP - 1)
+    def _(i):
+        combine(i)
+        combine(GROUP + i)
+
+    @pl.loop(0, 4)
+    def _(k):
+        part[k] = project(k, early)
+
+    combine(GROUP - 1)
+    combine(HEADS - 1)
+    neighbours = ((p, 1 - t, g), (p, 1 - t, 1 - g))
+    for k in (0, 1):
+        part_send[k] = (part[k] + project(k, late)).astype(BF)
+        send(part_send.at[k], part_recv.at[k], part_send_sem.at[k], part_recv_sem.at[k], neighbours[k])
+    for k in (2, 3):
+        part[k] = part[k] + project(k, late)
+
+    @pl.loop(0, GROUP)
+    def _(i):
+        for b in range(2):
             @pl.when(b != c)
             def _():
                 await_bytes(o_send.at[i, b], o_sem.at[i, b])
 
-    @pl.loop(0, HEADS)
-    def _(head):
-        await_bytes(attn.at[head], guide_send.at[head])
-
-    await_bytes(res_other, res_sem.at[0])
+        for b in range(2, 8):
+            await_bytes(o_send.at[i, b], o_sem.at[i, b])
+        await_bytes(attn.at[i], guide_send.at[i])
+        await_bytes(attn.at[GROUP + i], guide_send.at[GROUP + i])
+
+    for k in (0, 1):
+        columns = slice(k * HALF, (k + 1) * HALF)
+        await_bytes(part_recv.at[k], part_recv_sem.at[k])
+        proj = part[2 + k] + part_recv[k].astype(F32)
+        out[:, columns] = (base[:, columns] + gate[:, columns] * proj).astype(BF)
     for k in (0, 1):
         await_bytes(part_send.at[k], part_send_sem.at[k])
 
@@ -477,7 +500,8 @@
             pltpu.VMEM((4, width, HALF), BF),
             pltpu.VMEM((2, ROWS, HALF), BF),
             pltpu.VMEM((2, ROWS, HALF), BF),
-            pltpu.VMEM((2, ROWS, HALF), F32),
+            pltpu.VMEM((4, ROWS, HALF), F32),
+            pltpu.VMEM((ROWS, width), F32),
             pltpu.VMEM((ROWS, width), BF),
             pltpu.VMEM((ROWS, width), BF),
             pltpu.VMEM((steps, width), F32),
@@ -496,7 +520,7 @@
             dma((2,)),
             dma((2,)),
             dma((2,)),
-            dma((8,)),
+            dma((10,)),
         ],
         compiler_params=pltpu.CompilerParams(
             collective_id=0, has_side_effects=True, vmem_limit_bytes=56 * 1024 * 1024

time: 75 us -> 73.6 us (0.981)
  Pallas kernels: 71.7 us -> 70.3 us
    pallas_call x1, Pallas kernels: 71.7 us -> 70.3 us  [per_device(): pl.pallas_call(kernel, out_shape=jax.ShapeDtypeStruct((ROWS, width), BF),...]
where the time goes in v4:
time: 73.6 us; the launch traced here: 72.8 us
  Pallas kernels  70.3 us (96%)
  local copies, waits for them, and re-layouts  1.84 us (2%)
    pallas_call x1, Pallas kernels, per_device(): pl.pallas_call(kernel, out_shape=jax.ShapeDtypeStruct((ROWS, width), BF),...  70.3 us
    unnamed x1, local copies, waits for them, and re-layouts  1.84 us

profile of v4, /device:TPU:0, one launch (start us, length us, event | category | flops | bytes accessed | tf_op | source)
XLA Modules:
  0.0 72.8 jit_solution(7014488936890830995)
XLA Ops:
  0.7 70.3 %shard_map.109 = bf16[192,1280]{1,0:T(8,128)(2,1)} custom-call(bf16[1,192,1280]{2,1,0:T(8,128)(2,1)} %fresh_q.1, bf16[1,192,1280]{2,1,0:T(8,128)(2,1)} %fresh_k.1, bf16[1,192,1280]{2,1,0:T(8,128)(2,1)} %fresh_v.1, bf16[1,192,1280]{2,1,0:T(8,128)(2,1)} %stale_k.1, bf16[1,192,1280]{2,1,0:T(8,128)(2,1)} %stale_v.1, bf16[1,192,2560]{2,1,0:T(8,128)(2,1)} %residual.1, ...), custom_call_target="tpu_custom_call" | custom-call | flops 8000000000 | bytes 12000000 | tf_op jit(solution)/shard_map/pallas_call | solution.py:478
  71.0 1.8 %copy.14 = bf16[192,1280]{1,0:T(8,128)(2,1)} copy(bf16[192,1280]{1,0:T(8,128)(2,1)} %shard_map.109) | data formatting | bytes 983040

commit v5 on v4

--- a/solution.py
+++ b/solution.py
@@ -20,6 +20,8 @@
 HEADS = 10
 KEYS = 8 * ROWS
 NOTE = 16
+EARLY = 3
+LATE = GROUP - EARLY
 HALF = 640
 SCORE_SCALE = math.log2(math.e) / math.sqrt(HEAD_DIM)
 
@@ -59,10 +61,11 @@
 def kernel(
     fresh_q, fresh_k, fresh_v, stale_k, stale_v, residual, weight, gate_table, freqs, positions, timestep,
     out,
-    kb, vb, qb, scores_a, scores_b, weights_a, weights_b, q_raw, k_raw, q_rot, k_rot, o_send, o_recv, attn, attn_other, combined, w_tiles, part_send, part_recv,
+    kb, vb, qb, scores_a, scores_b, weights_a, weights_b, q_raw, k_raw, q_rot, k_rot, o_send, o_recv, attn, attn_other,
+    combined, combined_far, w_tiles, w_far, part_send, part_recv,
     part, base, res_own, res_other, gate_rows, cosines, sines,
     recv, o_recv_sem, kv_sem, q_sem, far_sem, sib_sem, local_sem, o_sem, guide_send, guide_recv, part_send_sem,
-    part_recv_sem, res_sem, load_sem,
+    part_recv_sem, res_sem, load_sem, w_sem, combined_send, combined_recv,
 ):
     p, t, g = lax.axis_index("patch"), lax.axis_index("tensor"), lax.axis_index("guide")
     x, y, c = p // (2 * RING), (p // 2) % RING, p % 2
@@ -240,6 +243,12 @@
         send_sibling_stale(i)
         local_stale(i, True)
 
+    neighbours = ((p, 1 - t, g), (p, 1 - t, 1 - g))
+    late_rows = tuple(slice((group * GROUP + EARLY) * HEAD_DIM, (group + 1) * GROUP * HEAD_DIM) for group in (0, 1))
+    early_rows = tuple(slice(group * GROUP * HEAD_DIM, (group * GROUP + EARLY) * HEAD_DIM) for group in (0, 1))
+    for k, branch in enumerate((g, 1 - g)):
+        theirs = pl.ds(pl.multiple_of((2 * (1 - t) + branch) * 2 * HALF, HEAD_DIM), 2 * HALF)
+        send(weight.at[late_rows[k], theirs], w_far.at[k], w_sem.at[k], w_sem.at[2 + k], neighbours[k])
     send(residual.at[0, :, partner], res_other, res_sem.at[0], res_sem.at[1], (p, t, 1 - g))
     width = 2 * HALF
     starts = (
@@ -347,6 +356,20 @@
             attn[head, first:last, :] = result.astype(BF)
         send(attn.at[head], attn_other.at[head], guide_send.at[head], guide_recv.at[head], (p, t, 1 - g))
 
+    own_share = (GUIDE_SCALE - (2 * GUIDE_SCALE - 1) * g).astype(F32)
+    other_share = (1.0 - GUIDE_SCALE + (2 * GUIDE_SCALE - 1) * g).astype(F32)
+
+    def combine(head):
+        await_bytes(attn_other.at[head], guide_recv.at[head])
+        both = own_share * attn[head].astype(F32) + other_share * attn_other[head].astype(F32)
+        combined[:, head_columns(head)] = both.astype(BF)
+
+    def project(k, spans):
+        first, second = (
+            jnp.dot(combined[:, span], w_tiles[k, span, :], preferred_element_type=F32) for span in spans
+        )
+        return first + second
+
     forward_queries(0)
     send_queries(2)
     forward_keys(0)
@@ -386,6 +409,17 @@
             merge(i - 1)
             merge(GROUP + i - 1)
 
+        @pl.when(i == EARLY + 1)
+        def _():
+            for copy in loads:
+                copy.wait()
+            for head in range(EARLY):
+                combine(head)
+                combine(GROUP + head)
+            for k in (0, 1):
+                part_send[k] = project(k, early_rows).astype(BF)
+                send(part_send.at[k], part_recv.at[k], part_send_sem.at[k], part_recv_sem.at[k], neighbours[k])
+
     @pl.loop(0, GROUP)
     def _(i):
         for k in range(8):
@@ -401,50 +435,43 @@
 
     for k in (3, 4):
         await_bytes(q_rot.at[0:GROUP], sib_sem.at[0, k])
-    for copy in loads:
-        copy.wait()
     await_bytes(res_other, res_sem.at[0])
     await_bytes(res_other, res_sem.at[1])
-    own_share = (GUIDE_SCALE - (2 * GUIDE_SCALE - 1) * g).astype(F32)
-    other_share = (1.0 - GUIDE_SCALE + (2 * GUIDE_SCALE - 1) * g).astype(F32)
     base[...] = own_share * res_own[...].astype(F32) + other_share * res_other[...].astype(F32)
     steps = lax.broadcasted_iota(jnp.int32, gate_rows.shape, 0)
     gate = jnp.sum(jnp.where(steps == timestep[0], gate_rows[...], 0.0), axis=0, keepdims=True)
 
+    def exchange(j):
+        for group in (0, 1):
+            head = group * GROUP + EARLY + j
+            combine(head)
+            send(
+                combined.at[:, head * HEAD_DIM : (head + 1) * HEAD_DIM],
+                combined_far.at[group, :, j * HEAD_DIM : (j + 1) * HEAD_DIM],
+                combined_send.at[group, j],
+                combined_recv.at[group, j],
+                neighbours[group],
+            )
+
+    for j in range(LATE - 2):
+        exchange(j)
     merge(GROUP - 1)
     merge(2 * GROUP - 1)
-
-    def combine(head):
-        await_bytes(attn_other.at[head], guide_recv.at[head])
-        both = own_share * attn[head].astype(F32) + other_share * attn_other[head].astype(F32)
-        combined[:, head_columns(head)] = both.astype(BF)
-
-    late = (slice((GROUP - 1) * HEAD_DIM, GROUP * HEAD_DIM), slice((HEADS - 1) * HEAD_DIM, HEADS * HEAD_DIM))
-    early = (slice(0, (GROUP - 1) * HEAD_DIM), slice(GROUP * HEAD_DIM, (HEADS - 1) * HEAD_DIM))
-
-    def project(k, spans):
-        first, second = (
-            jnp.dot(combined[:, span], w_tiles[k, span, :], preferred_element_type=F32) for span in spans
-        )
-        return first + second
-
-    @pl.loop(0, GROUP - 1)
-    def _(i):
-        combine(i)
-        combine(GROUP + i)
-
-    @pl.loop(0, 4)
+    exchange(LATE - 2)
+
+    @pl.loop(2, 4)
     def _(k):
-        part[k] = project(k, early)
-
-    combine(GROUP - 1)
-    combine(HEADS - 1)
-    neighbours = ((p, 1 - t, g), (p, 1 - t, 1 - g))
+        part[k - 2] = project(k, early_rows)
+
+    exchange(LATE - 1)
+
+    @pl.loop(2, 4)
+    def _(k):
+        part[k - 2] += project(k, late_rows)
+
     for k in (0, 1):
-        part_send[k] = (part[k] + project(k, late)).astype(BF)
-        send(part_send.at[k], part_recv.at[k], part_send_sem.at[k], part_recv_sem.at[k], neighbours[k])
-    for k in (2, 3):
-        part[k] = part[k] + project(k, late)
+        await_bytes(w_far.at[k], w_sem.at[k])
+        await_bytes(w_far.at[k], w_sem.at[2 + k])
 
     @pl.loop(0, GROUP)
     def _(i):
@@ -459,12 +486,21 @@
         await_bytes(attn.at[GROUP + i], guide_send.at[GROUP + i])
 
     for k in (0, 1):
+        await_bytes(part_recv.at[k], part_recv_sem.at[k])
+    for group in (0, 1):
+        for j in range(LATE):
+            await_bytes(combined_far.at[group, :, j * HEAD_DIM : (j + 1) * HEAD_DIM], combined_recv.at[group, j])
+    for k in (0, 1):
         columns = slice(k * HALF, (k + 1) * HALF)
-        await_bytes(part_recv.at[k], part_recv_sem.at[k])
-        proj = part[2 + k] + part_recv[k].astype(F32)
+        proj = part[k] + part_recv[k].astype(F32)
+        for group in (0, 1):
+            proj = proj + jnp.dot(combined_far[group], w_far[group, :, columns], preferred_element_type=F32)
         out[:, columns] = (base[:, columns] + gate[:, columns] * proj).astype(BF)
     for k in (0, 1):
         await_bytes(part_send.at[k], part_send_sem.at[k])
+    for group in (0, 1):
+        for j in range(LATE):
+            await_bytes(attn.at[0], combined_send.at[group, j])
 
 
 def per_device(
@@ -497,10 +533,12 @@
             pltpu.VMEM((HEADS, ROWS, HEAD_DIM), BF),
             pltpu.VMEM((HEADS, ROWS, HEAD_DIM), BF),
             pltpu.VMEM((ROWS, width), BF),
+            pltpu.VMEM((2, ROWS, LATE * HEAD_DIM), BF),
             pltpu.VMEM((4, width, HALF), BF),
+            pltpu.VMEM((2, LATE * HEAD_DIM, width), BF),
             pltpu.VMEM((2, ROWS, HALF), BF),
             pltpu.VMEM((2, ROWS, HALF), BF),
-            pltpu.VMEM((4, ROWS, HALF), F32),
+            pltpu.VMEM((2, ROWS, HALF), F32),
             pltpu.VMEM((ROWS, width), F32),
             pltpu.VMEM((ROWS, width), BF),
             pltpu.VMEM((ROWS, width), BF),
@@ -521,6 +559,9 @@
             dma((2,)),
             dma((2,)),
             dma((10,)),
+            dma((4,)),
+            dma((2, LATE)),
+            dma((2, LATE)),
         ],
         compiler_params=pltpu.CompilerParams(
             collective_id=0, has_side_effects=True, vmem_limit_bytes=56 * 1024 * 1024

time: 73.6 us -> 72 us (0.978)
  Pallas kernels: 70.3 us -> 69.3 us
    pallas_call x1, Pallas kernels: 70.3 us -> 69.3 us  [per_device(): pl.pallas_call(kernel, out_shape=jax.ShapeDtypeStruct((ROWS, width), BF),...]
where the time goes in v5:
time: 72 us; the launch traced here: 71.8 us
  Pallas kernels  69.3 us (96%)
  local copies, waits for them, and re-layouts  1.84 us (3%)
    pallas_call x1, Pallas kernels, per_device(): pl.pallas_call(kernel, out_shape=jax.ShapeDtypeStruct((ROWS, width), BF),...  69.3 us
    unnamed x1, local copies, waits for them, and re-layouts  1.84 us

profile of v5, /device:TPU:0, one launch (start us, length us, event | category | flops | bytes accessed | tf_op | source)
XLA Modules:
  0.0 71.8 jit_solution(4173329695692939285)
XLA Ops:
  0.7 69.3 %shard_map.109 = bf16[192,1280]{1,0:T(8,128)(2,1)} custom-call(bf16[1,192,1280]{2,1,0:T(8,128)(2,1)} %fresh_q.1, bf16[1,192,1280]{2,1,0:T(8,128)(2,1)} %fresh_k.1, bf16[1,192,1280]{2,1,0:T(8,128)(2,1)} %fresh_v.1, bf16[1,192,1280]{2,1,0:T(8,128)(2,1)} %stale_k.1, bf16[1,192,1280]{2,1,0:T(8,128)(2,1)} %stale_v.1, bf16[1,192,2560]{2,1,0:T(8,128)(2,1)} %residual.1, ...), custom_call_target="tpu_custom_call" | custom-call | flops 8000000000 | bytes 12000000 | tf_op jit(solution)/shard_map/pallas_call | solution.py:514
  69.9 1.8 %copy.14 = bf16[192,1280]{1,0:T(8,128)(2,1)} copy(bf16[192,1280]{1,0:T(8,128)(2,1)} %shard_map.109) | data formatting | bytes 983040

commit v6 on v5

--- a/solution.py
+++ b/solution.py
@@ -269,8 +269,6 @@
             gate_table.at[:, pl.ds(pl.multiple_of((2 * t + g) * width, HEAD_DIM), width)], gate_rows, load_sem.at[7]
         )
     )
-    for copy in loads:
-        copy.start()
 
     def pieces(chip):
         if chip:
@@ -403,6 +401,11 @@
             if n >= 2:
                 send_back(i, 2 * order[n - 2])
                 send_back(i, 2 * order[n - 2] + 1)
+
+        @pl.when(i == 0)
+        def _():
+            for copy in loads:
+                copy.start()
 
         @pl.when(i > 0)
         def _():

time: 72 us -> 72 us (level)
  no operation moved by 1% of the time
where the time goes in v6:
time: 72 us; the launch traced here: 71.8 us
  Pallas kernels  69.3 us (96%)
  local copies, waits for them, and re-layouts  1.84 us (3%)
    pallas_call x1, Pallas kernels, per_device(): pl.pallas_call(kernel, out_shape=jax.ShapeDtypeStruct((ROWS, width), BF),...  69.3 us
    unnamed x1, local copies, waits for them, and re-layouts  1.84 us

profile of v6, /device:TPU:0, one launch (start us, length us, event | category | flops | bytes accessed | tf_op | source)
XLA Modules:
  0.0 71.8 jit_solution(96358911985191461)
XLA Ops:
  0.7 69.3 %shard_map.109 = bf16[192,1280]{1,0:T(8,128)(2,1)} custom-call(bf16[1,192,1280]{2,1,0:T(8,128)(2,1)} %fresh_q.1, bf16[1,192,1280]{2,1,0:T(8,128)(2,1)} %fresh_k.1, bf16[1,192,1280]{2,1,0:T(8,128)(2,1)} %fresh_v.1, bf16[1,192,1280]{2,1,0:T(8,128)(2,1)} %stale_k.1, bf16[1,192,1280]{2,1,0:T(8,128)(2,1)} %stale_v.1, bf16[1,192,2560]{2,1,0:T(8,128)(2,1)} %residual.1, ...), custom_call_target="tpu_custom_call" | custom-call | flops 8000000000 | bytes 12000000 | tf_op jit(solution)/shard_map/pallas_call | solution.py:517
  70.0 1.8 %copy.14 = bf16[192,1280]{1,0:T(8,128)(2,1)} copy(bf16[192,1280]{1,0:T(8,128)(2,1)} %shard_map.109) | data formatting | bytes 983040
